TPU v7x, 32 devices: a whole 2x2x4 slice. The times are simulated.
32 devices in a mesh: row: 4 (over z), col: 8 (over y, x, core).
Axes of the slice: x: 2, y: 2, z: 4, core: 2. Of those that a mesh axis runs over, the one named last changes fastest.
Arguments:
- src_pos: float32 [3, 65536], P(None, 'row'), may hold values from 0 to 10
- tgt_pos: float32 [3, 2048], P(None, 'col'), may hold values from 0 to 20
- src_weight: float32 [65536], P('row'), may hold values from 0.1 to 3
- tgt_weight: float32 [2048], P('col'), may hold values from 0.1 to 3
- src_order: int32 [65536], P('row'), may hold values from 0 to 65535, as said below
- tgt_order: int32 [2048], P('col'), may hold values from 0 to 2047, as said below
- tile_mask: int32 [256, 8], P('row', 'col'), may hold values from 0 to 1, as said below
Outputs:
- src_potential: float32 [65536], P('row')
- tgt_potential: float32 [2048], P('col')
- displacement: float32 [3, 65536], P(None, 'row')
Inputs may be any that keep to these rules, and one draw needn't show every extreme that they name: `src_order`: each aligned block of 16384 entries is a permutation of that block's own indices. `tgt_order`: each aligned block of 256 entries is a permutation of that block's own indices. `tile_mask`: every row and every column of the mask holds at least one kept pair.
All inputs are finite; a program needn't handle non-finite values.
Results may differ from a plain program's by a relative error of at most 0.0003.
Values sent between devices are 32-bit elements; how exact they have to be, the bound alone decides.
A program may use at most 64 MiB of HBM per device.

v0:
```python
import jax
import jax.numpy as jnp
from jax import lax
from jax.sharding import PartitionSpec as P

TILE = 256
SWEEPS = 2


epsilon = 0.4
lowest = -1e30
block_limit = 1 << 20


def merged_2(part, axis, combine):
    gathered = jax.tree.map(lambda a: lax.all_gather(a, axis), part)

    def take(source):
        return jax.tree.map(lambda a: lax.dynamic_index_in_dim(a, source, 0, False), gathered)

    return lax.fori_loop(
        1, lax.axis_size(axis), lambda source, state: combine(state, take(source)), take(0)
    )


def tile_pass(sources, targets, src_terms, tgt_terms, keep_mask, with_shift):
    rows_here = sources.shape[1]
    cols_here = targets.shape[1]
    src_tiles = rows_here // TILE
    tgt_tiles = cols_here // TILE
    block_tiles = max(1, min(src_tiles, block_limit // (TILE * cols_here)))
    while src_tiles % block_tiles != 0:
        block_tiles = block_tiles - 1
    block_rows = block_tiles * TILE
    blocks = src_tiles // block_tiles
    src_split = sources.reshape(3, blocks, block_rows).transpose(1, 0, 2)
    term_split = src_terms.reshape(blocks, block_rows)
    mask_split = keep_mask.reshape(blocks, block_tiles, tgt_tiles)

    def visit(carried, slices):
        col_top, col_sum = carried
        src_block, term_block, mask_block = slices
        distance = 0.5 * sum(
            (
                (src_block[coordinate][:, None] - targets[coordinate][None, :]) ** 2
                for coordinate in range(3)
            )
        )
        scaled = distance / epsilon
        alive = jnp.broadcast_to(
            (mask_block > 0)[:, None, :, None], (block_tiles, TILE, tgt_tiles, TILE)
        ).reshape(block_rows, cols_here)
        toward = tgt_terms[None, :] - scaled
        backward = term_block[:, None] - scaled
        row_top = jnp.max(jnp.where(alive, toward, lowest), axis=1)
        row_exp = jnp.where(alive, jnp.exp(toward - row_top[:, None]), 0.0)
        row_sum = jnp.sum(row_exp, axis=1)
        if with_shift:
            pulled = jnp.dot(row_exp, targets.T, precision=lax.Precision.HIGHEST).T
        else:
            pulled = jnp.zeros((3, block_rows), jnp.float32)
        col_peak = jnp.max(jnp.where(alive, backward, lowest), axis=0)
        renewed = jnp.maximum(col_top, col_peak)
        col_sum = col_sum * jnp.exp(col_top - renewed) + jnp.sum(
            jnp.where(alive, jnp.exp(backward - renewed[None, :]), 0.0), axis=0
        )
        return ((renewed, col_sum), (row_top, row_sum, pulled))

    starting = (jnp.full((cols_here,), lowest, jnp.float32), jnp.zeros((cols_here,), jnp.float32))
    (col_top, col_sum), (row_top, row_sum, pulled) = lax.scan(
        visit, starting, (src_split, term_split, mask_split)
    )
    return (
        row_top.reshape(-1),
        row_sum.reshape(-1),
        pulled.transpose(1, 0, 2).reshape(3, -1),
        col_top,
        col_sum,
    )


def merge_rule(scaled_count):

    def combine(left_part, right_part):
        peak_value = jnp.maximum(left_part[0], right_part[0])
        left_scale = jnp.exp(left_part[0] - peak_value)
        right_scale = jnp.exp(right_part[0] - peak_value)
        merged = [peak_value]
        for member in range(1, 1 + scaled_count):
            merged.append(left_part[member] * left_scale + right_part[member] * right_scale)
        for member in range(1 + scaled_count, len(left_part)):
            merged.append(left_part[member] + right_part[member])
        return tuple(merged)

    return combine


def potential(peak_value, total_sum, mass_total):
    return -epsilon * (peak_value + jnp.log(total_sum) - jnp.log(mass_total))


def local(src_pos, tgt_pos, src_weight, tgt_weight, src_order, tgt_order, tile_mask):
    rows_here = src_pos.shape[1]
    cols_here = tgt_pos.shape[1]
    row_at = lax.axis_index("row")
    col_at = lax.axis_index("col")
    targets = jnp.take(tgt_pos, tgt_order - col_at * cols_here, axis=1)
    tgt_mass = jnp.take(tgt_weight, tgt_order - col_at * cols_here)
    passes = SWEEPS + 2
    src_total = lax.psum(jnp.sum(src_weight), "row")
    sources = jnp.take(src_pos, src_order - row_at * rows_here, axis=1)
    src_mass = jnp.take(src_weight, src_order - row_at * rows_here)
    tgt_total = lax.psum(jnp.sum(tgt_mass), "col")
    log_src = jnp.log(src_mass)
    log_tgt = jnp.log(tgt_mass)
    src_field = jnp.zeros((rows_here,), jnp.float32)
    tgt_field = jnp.zeros((cols_here,), jnp.float32)
    for sweep_at in range(passes):
        closing = sweep_at == passes - 1
        partial_value = tile_pass(
            sources,
            targets,
            log_src + src_field / epsilon,
            log_tgt + tgt_field / epsilon,
            tile_mask,
            closing,
        )
        row_part = (partial_value[0], partial_value[1])
        if closing:
            row_part = row_part + (partial_value[2],)
        scaled_count = len(row_part) - 1
        col_part = (partial_value[3], partial_value[4])
        row_done = merged_2(row_part, "col", merge_rule(scaled_count))
        col_done = merged_2(col_part, "row", merge_rule(1))
        src_new = potential(row_done[0], row_done[1], tgt_total)
        tgt_new = potential(col_done[0], col_done[1], src_total)
        if sweep_at == 0 or closing:
            src_field, tgt_field = (src_new, tgt_new)
        else:
            src_field = 0.5 * (src_field + src_new)
            tgt_field = 0.5 * (tgt_field + tgt_new)
        if closing:
            displacement = sources - row_done[2] / row_done[1][None, :]
    return (src_field, tgt_field, displacement)


def solution(mesh):
    in_specs = (
        P(None, "row"),
        P(None, "col"),
        P("row"),
        P("col"),
        P("row"),
        P("col"),
        P("row", "col"),
    )
    out_specs = (P("row"), P("col"), P(None, "row"))
    return jax.shard_map(local, mesh=mesh, in_specs=in_specs, out_specs=out_specs, check_vma=False)
```

profile of v0, /device:TPU:0, one launch (start us, length us, event | category | flops | bytes accessed | tf_op | source)
XLA Modules:
  0.0 550.3 jit_solution(14705456542853913274)
XLA Ops:
  14.7 57.8 %gather_fusion.1 = f32[16384,3]{1,0:T(8,128)} fusion(f32[3,16384]{0,1:T(8,128)} %copy.82, s32[16384]{0:T(1024)S(1)} %fusion.46), kind=kCustom, calls=%fused_computation.1 | custom fusion | bytes 458752 | tf_op jit(solution)/shard_map/jit(_take)/gather | solution.py:111
  78.0 90.5 %gather_fusion = f32[16384]{0:T(1024)S(1)} fusion(f32[16384]{0:T(1024)S(1)} %copy-done.1, s32[16384]{0:T(1024)S(1)} %fusion.46), kind=kCustom, calls=%fused_computation | custom fusion | bytes 196608 | tf_op jit(solution)/shard_map/jit(_take)/gather | solution.py:112
  173.1 35.1 %while.224 = (s32[]{:T(128)}, f32[256]{0:T(256)S(1)}, f32[256]{0:T(256)S(1)}, f32[4,4096]{1,0:T(4,128)S(1)}, f32[4,4096]{1,0:T(4,128)S(1)}, /*index=5*/s32[4,16,...) while((s32[]{:T(128)}, f32[256]{0:T(256)S(1)}, ...), condition=%wide.region_5.6_spmd.clone, body=%wide.region_0.5_spmd.clone.sunk | while | flops 33547540 | bytes 601396 | solution.py:70
  208.3 12.7 %all-gather.10 = f32[4,1,256]{2,1,0:T(1,128)S(1)} all-gather(f32[1,1,256]{2,1,0:T(1,128)S(1)} %bitcast.330), channel_id=2, replica_groups=mesh['row'=4,'col'=8] {'row'}, dimensions={0}, use_global_device_ids=true | all-gather | bytes 5120 | tf_op jit(solution)/shard_map/all_gather | solution.py:16
  228.7 9.9 %all-gather.8 = f32[8,1,16384]{2,1,0:T(1,128)S(1)} all-gather(f32[1,1,16384]{2,1,0:T(1,128)S(1)} %reshape.1404), channel_id=1, replica_groups=mesh['row'=4,'col'=8] {'col'}, dimensions={0}, use_global_device_ids=true | all-gather | bytes 589824 | tf_op jit(solution)/shard_map/all_gather | solution.py:16
  239.0 9.8 %all-gather.9 = f32[8,1,16384]{2,1,0:T(1,128)S(1)} all-gather(f32[1,1,16384]{2,1,0:T(1,128)S(1)} %reshape.1406), channel_id=1, replica_groups=mesh['row'=4,'col'=8] {'col'}, dimensions={0}, use_global_device_ids=true | all-gather | bytes 589824 | tf_op jit(solution)/shard_map/all_gather | solution.py:16
  250.5 11.0 %psum.15 = f32[]{:T(128)} all-reduce(f32[]{:T(128)} %reduce_sum.103), channel_id=1, replica_groups=mesh['row'=4,'col'=8] {'row'}, use_global_device_ids=true, to_apply=%region_13.14 | all-reduce | flops 1 | bytes 8 | tf_op jit(solution)/shard_map/psum | solution.py:110
  263.4 12.4 %psum.14 = f32[]{:T(128)} all-reduce(f32[]{:T(128)} %select_reduce_fusion.16), channel_id=1, replica_groups=mesh['row'=4,'col'=8] {'col'}, use_global_device_ids=true, to_apply=%region_9.10 | all-reduce | flops 1 | bytes 8 | tf_op jit(solution)/shard_map/psum | solution.py:113
  276.7 35.1 %while.225 = (s32[]{:T(128)}, f32[256]{0:T(256)S(1)}, f32[256]{0:T(256)S(1)}, f32[4,4096]{1,0:T(4,128)S(1)}, f32[4,4096]{1,0:T(4,128)S(1)}, /*index=5*/s32[4,16,...) while((s32[]{:T(128)}, f32[256]{0:T(256)S(1)}, ...), condition=%wide.region_19.20_spmd.clone, body=%wide.region_14.19_spmd.clone.sunk | while | flops 33547540 | bytes 601396 | solution.py:70
  311.8 7.6 %all-gather.14 = f32[4,1,256]{2,1,0:T(1,128)S(1)} all-gather(f32[1,1,256]{2,1,0:T(1,128)S(1)} %bitcast.329), channel_id=4, replica_groups=mesh['row'=4,'col'=8] {'row'}, dimensions={0}, use_global_device_ids=true | all-gather | bytes 5120 | tf_op jit(solution)/shard_map/all_gather | solution.py:16
  319.4 9.6 %all-gather.15 = f32[4,1,256]{2,1,0:T(1,128)S(1)} all-gather(f32[1,1,256]{2,1,0:T(1,128)S(1)} %bitcast.376), channel_id=5, replica_groups=mesh['row'=4,'col'=8] {'row'}, dimensions={0}, use_global_device_ids=true | all-gather | bytes 5120 | tf_op jit(solution)/shard_map/all_gather | solution.py:16
  329.0 8.9 %all-gather.12 = f32[8,1,16384]{2,1,0:T(1,128)S(1)} all-gather(f32[1,1,16384]{2,1,0:T(1,128)S(1)} %reshape.1412), channel_id=1, replica_groups=mesh['row'=4,'col'=8] {'col'}, dimensions={0}, use_global_device_ids=true | all-gather | bytes 589824 | tf_op jit(solution)/shard_map/all_gather | solution.py:16
  338.4 10.0 %all-gather.13 = f32[8,1,16384]{2,1,0:T(1,128)S(1)} all-gather(f32[1,1,16384]{2,1,0:T(1,128)S(1)} %reshape.1414), channel_id=1, replica_groups=mesh['row'=4,'col'=8] {'col'}, dimensions={0}, use_global_device_ids=true | all-gather | bytes 589824 | tf_op jit(solution)/shard_map/all_gather | solution.py:16
  350.4 35.1 %while.226 = (s32[]{:T(128)}, f32[256]{0:T(256)S(1)}, f32[256]{0:T(256)S(1)}, f32[4,4096]{1,0:T(4,128)S(1)}, f32[4,4096]{1,0:T(4,128)S(1)}, /*index=5*/s32[4,16,...) while((s32[]{:T(128)}, f32[256]{0:T(256)S(1)}, ...), condition=%wide.region_29.30_spmd.clone, body=%wide.region_24.29_spmd.clone.sunk | while | flops 33547540 | bytes 601396 | solution.py:70
  385.5 7.6 %all-gather.18 = f32[4,1,256]{2,1,0:T(1,128)S(1)} all-gather(f32[1,1,256]{2,1,0:T(1,128)S(1)} %bitcast.328), channel_id=6, replica_groups=mesh['row'=4,'col'=8] {'row'}, dimensions={0}, use_global_device_ids=true | all-gather | bytes 5120 | tf_op jit(solution)/shard_map/all_gather | solution.py:16
  393.1 9.6 %all-gather.19 = f32[4,1,256]{2,1,0:T(1,128)S(1)} all-gather(f32[1,1,256]{2,1,0:T(1,128)S(1)} %bitcast.375), channel_id=7, replica_groups=mesh['row'=4,'col'=8] {'row'}, dimensions={0}, use_global_device_ids=true | all-gather | bytes 5120 | tf_op jit(solution)/shard_map/all_gather | solution.py:16
  402.8 8.9 %all-gather.16 = f32[8,1,16384]{2,1,0:T(1,128)S(1)} all-gather(f32[1,1,16384]{2,1,0:T(1,128)S(1)} %reshape.1420), channel_id=1, replica_groups=mesh['row'=4,'col'=8] {'col'}, dimensions={0}, use_global_device_ids=true | all-gather | bytes 589824 | tf_op jit(solution)/shard_map/all_gather | solution.py:16
  412.2 9.8 %all-gather.17 = f32[8,1,16384]{2,1,0:T(1,128)S(1)} all-gather(f32[1,1,16384]{2,1,0:T(1,128)S(1)} %reshape.1422), channel_id=1, replica_groups=mesh['row'=4,'col'=8] {'col'}, dimensions={0}, use_global_device_ids=true | all-gather | bytes 589824 | tf_op jit(solution)/shard_map/all_gather | solution.py:16
  424.0 67.9 %while.227 = (s32[]{:T(128)}, f32[256]{0:T(256)S(1)}, f32[256]{0:T(256)S(1)}, f32[4,4096]{1,0:T(4,128)S(1)}, f32[4,4096]{1,0:T(4,128)S(1)}, /*index=5*/f32[4,3,4...) while((s32[]{:T(128)}, f32[256]{0:T(256)S(1)}, ...), condition=%wide.region_39.40_spmd.clone, body=%wide.region_34.39_spmd.clone.sunk | while | flops 83879184 | bytes 838496 | solution.py:70
  492.0 10.3 %all-gather.20 = f32[8,1,16384]{2,1,0:T(1,128)S(1)} all-gather(f32[1,1,16384]{2,1,0:T(1,128)S(1)} %reshape.1428), channel_id=1, replica_groups=mesh['row'=4,'col'=8] {'col'}, dimensions={0}, use_global_device_ids=true | all-gather | bytes 589824 | tf_op jit(solution)/shard_map/all_gather | solution.py:16
  502.7 10.8 %all-gather.21 = f32[8,1,16384]{2,1,0:T(1,128)S(1)} all-gather(f32[1,1,16384]{2,1,0:T(1,128)S(1)} %reshape.1430), channel_id=1, replica_groups=mesh['row'=4,'col'=8] {'col'}, dimensions={0}, use_global_device_ids=true | all-gather | bytes 589824 | tf_op jit(solution)/shard_map/all_gather | solution.py:16
  513.8 7.6 %all-gather.22 = f32[4,1,256]{2,1,0:T(1,128)S(1)} all-gather(f32[1,1,256]{2,1,0:T(1,128)S(1)} %bitcast.327), channel_id=8, replica_groups=mesh['row'=4,'col'=8] {'row'}, dimensions={0}, use_global_device_ids=true | all-gather | bytes 5120 | tf_op jit(solution)/shard_map/all_gather | solution.py:16
  521.3 9.6 %all-gather.23 = f32[4,1,256]{2,1,0:T(1,128)S(1)} all-gather(f32[1,1,256]{2,1,0:T(1,128)S(1)} %bitcast.374), channel_id=9, replica_groups=mesh['row'=4,'col'=8] {'row'}, dimensions={0}, use_global_device_ids=true | all-gather | bytes 5120 | tf_op jit(solution)/shard_map/all_gather | solution.py:16
  532.6 9.3 %while.222 = (s32[]{:T(128)}, f32[16384]{0:T(1024)S(1)}, f32[16384]{0:T(1024)S(1)}, f32[3,16384]{1,0:T(4,128)S(1)}, f32[8,16384]{1,0:T(8,128)S(1)}, /*index=5*/f...) while((s32[]{:T(128)}, f32[16384]{0:T(1024)S(1)}, ...), condition=%wide.region_41.42_spmd, body=%wide.region_40.41_spmd.sunk | while | flops 245765 | bytes 1507479 | solution.py:21
  (493 shorter events, 221.5 us)
Async XLA Ops:
  7.2 161.6 %copy-start = (f32[256]{0:T(256)S(1)}, f32[256]{0:T(256)}, u32[]{:S(2)}) copy-start(f32[256]{0:T(256)} %param.34) | copy-start | bytes 3076
  7.2 524.5 %all-gather.26.cloned.1.call-start = ((), (), s32[]{:S(2)}) async-start(), calls=%async_computation | async-start | bytes 2359296 | tf_op jit(solution)/shard_map/all_gather | solution.py:16
  72.4 5.5 %copy-start.1 = (f32[16384]{0:T(1024)S(1)}, f32[16384]{0:T(1024)}, u32[]{:S(2)}) copy-start(f32[16384]{0:T(1024)} %param.33) | copy-start | bytes 196612
  77.9 90.8 %copy-start.4 = (s32[256]{0:T(256)S(1)}, s32[256]{0:T(256)}, u32[]{:S(2)}) copy-start(s32[256]{0:T(256)} %param.36) | copy-start | bytes 3076
  78.0 92.8 %copy-start.3 = (f32[3,256]{1,0:T(4,128)S(1)}, f32[3,256]{1,0:T(4,128)}, u32[]{:S(2)}) copy-start(f32[3,256]{1,0:T(4,128)} %param.32) | copy-start | bytes 9220
  78.0 94.4 %copy-start.5 = (s32[64,1]{0,1:T(1,128)S(1)}, s32[64,1]{0,1:T(1,128)}, u32[]{:S(2)}) copy-start(s32[64,1]{0,1:T(1,128)} %param.37) | copy-start | bytes 772
  208.2 68.3 %copy-start.2 = (s32[16384]{0:T(1024)S(1)}, s32[16384]{0:T(1024)}, u32[]{:S(2)}) copy-start(s32[16384]{0:T(1024)} %param.35) | copy-start | bytes 196612
Sparse Core Ops, SparseCore 0:
  492.0 25.9 all-gather.25
where the time goes:
time: 551 us; the launch traced here: 550 us
  local copies, waits for them, and re-layouts  187 us (34%)
  blocking collectives  174 us (32%)
  other arithmetic  142 us (26%)
  matrix products  27.8 us (5%)
  between operations  15.9 us (3%)
    all_gather x16, blocking collectives, merged_2(): gathered = jax.tree.map(lambda a: lax.all_gather(a, axis), part)  150 us
    gather x2, local copies, waits for them, and re-layouts, local(): src_mass = jnp.take(src_weight, src_order - row_at * rows_here)  90.6 us
    reduce_sum x16, other arithmetic, visit(): row_sum = jnp.sum(row_exp, axis=1)  66.9 us
    gather x2, local copies, waits for them, and re-layouts, local(): sources = jnp.take(src_pos, src_order - row_at * rows_here, axis=1)  63.2 us
    reduce_max x16, other arithmetic, visit(): row_top = jnp.max(jnp.where(alive, toward, lowest), axis=1)  58.5 us
    dot_general x4, matrix products, visit(): pulled = jnp.dot(row_exp, targets.T, precision=lax.Precision.HIGHEST).T  27.8 us
    psum x1, blocking collectives, local(): tgt_total = lax.psum(jnp.sum(tgt_mass), 'col')  12.4 us
  transfers between devices with their start and end apart: 1, of which 0 were waited for; matrix products, arithmetic and copies ran while one was open for 0% of the time, Pallas kernels for 0%

commit v1 on v0

v1 whole, which is shorter than its diff:
```python
import functools
import math

import jax
import jax.numpy as jnp
from jax import lax
from jax.experimental import pallas as pl
from jax.experimental.pallas import tpu as pltpu
from jax.sharding import PartitionSpec as P

TILE = 256
SWEEPS = 2
LANES = 128
FEATURES = 32

epsilon = 0.4
lowest = -1e30
middle = 5.0
log2e = math.log2(math.e)
scale = 0.5 * log2e / epsilon
MESH = pl.DeviceIdType.MESH


def rounded(x):
    return x.astype(jnp.bfloat16).astype(jnp.float32)


def three(x):
    high = rounded(x)
    mid = rounded(x - high)
    return high, mid, rounded(x - high - mid)


def columns_of(row):
    return jnp.broadcast_to(row, (LANES, row.shape[1])).T


def kernel(
    rows, cols,
    src_pos, src_weight, src_order, tgt_pos, tgt_weight, tgt_order, mask,
    src_out, tgt_out, move_out,
    table, feature, tgt_parts, tgt_feature, points, masses, cost, term, place,
    col_top, col_sum, field, own, moved,
    send_0, send_1, send_2, send_3, take_0, take_1, take_2, take_3, col_send, col_take,
    part_out, part_in, whole_out, whole_in, cross_out, cross_in,
):
    row_at = lax.axis_index("row")
    col_at = lax.axis_index("col")
    sends = (send_0, send_1, send_2, send_3)
    takes = (take_0, take_1, take_2, take_3)
    groups = src_order.shape[0]
    width = tgt_pos.shape[1]
    spans = width // LANES
    owned = field.shape[2]
    chunk = min(8, owned)
    pieces = owned // chunk
    passes = SWEEPS + 2

    barrier = pltpu.get_barrier_semaphore()
    for step in range(1, cols):
        pl.semaphore_signal(
            barrier, inc=1, device_id=(row_at, lax.rem(col_at + step, cols)), device_id_type=MESH
        )
    for step in range(1, rows):
        pl.semaphore_signal(
            barrier, inc=1, device_id=(lax.rem(row_at + step, rows), col_at), device_id_type=MESH
        )

    for entry in range(4):
        value = tgt_weight[...] if entry == 3 else tgt_pos[entry:entry + 1, :] - middle
        for at, part in enumerate(three(value)):
            tgt_parts[4 * at + entry:4 * at + entry + 1, :] = part
    tgt_parts[12:16, :] = jnp.zeros((4, width), jnp.float32)
    chosen = lax.broadcasted_iota(jnp.int32, (width, width), 0) == tgt_order[...] - col_at * width
    picked = jnp.dot(
        tgt_parts[...].astype(jnp.bfloat16),
        chosen.astype(jnp.float32).astype(jnp.bfloat16),
        preferred_element_type=jnp.float32,
    )
    picked = picked[0:4] + picked[4:8] + picked[8:12]
    tgt_feature[...] = jnp.zeros(tgt_feature.shape, jnp.float32)
    norm = jnp.zeros((1, width), jnp.float32)
    for axis in range(3):
        y = picked[axis:axis + 1]
        norm = norm - scale * y * y
        high, mid, low = three(2.0 * scale * y)
        for at, part in enumerate((high, mid, high, low, high, mid)):
            tgt_feature[6 * axis + at:6 * axis + at + 1, :] = part
        place[axis] = columns_of(y)
    for at, part in enumerate(three(norm)):
        tgt_feature[18 + at:19 + at, :] = part
    tgt_feature[21:25, :] = jnp.ones((4, width), jnp.float32)
    tgt_log = jnp.log2(picked[3:4])
    term[...] = columns_of(tgt_log)
    tgt_side = tgt_feature[...].T[:, :FEATURES].astype(jnp.bfloat16)
    tgt_local = jnp.sum(tgt_weight[...], axis=1, keepdims=True)
    src_local = jnp.sum(jnp.sum(src_weight[...], axis=1, keepdims=True), axis=0, keepdims=True)

    for entry in range(4):
        value = src_weight[...] if entry == 3 else src_pos[entry] - middle
        value = value.T
        high = rounded(value)
        span = slice(entry * LANES, (entry + 1) * LANES)
        table[span, 0:groups] = high.astype(jnp.bfloat16)
        table[span, groups:2 * groups] = (value - high).astype(jnp.bfloat16)
    feature[...] = jnp.zeros(feature.shape, jnp.float32)
    batch = feature.shape[1] // LANES

    def fetch(at, carried):
        index = jnp.concatenate(
            [src_order[pl.ds(at * batch + g, 1), :] for g in range(batch)], axis=1
        ) - row_at * (groups * LANES)
        lanes = batch * LANES
        high_at = lax.shift_right_logical(index, 7)
        low_at = lax.bitwise_and(index, LANES - 1)
        hot = lax.broadcasted_iota(jnp.int32, (groups, lanes), 0) == high_at
        hot = hot.astype(jnp.float32).astype(jnp.bfloat16)
        found = jnp.dot(
            table[...], jnp.concatenate([hot, hot], axis=0), preferred_element_type=jnp.float32
        )
        near = lax.broadcasted_iota(jnp.int32, (LANES, lanes), 0) == low_at
        values = [
            jnp.sum(
                jnp.where(near, found[entry * LANES:(entry + 1) * LANES], 0.0),
                axis=0, keepdims=True,
            )
            for entry in range(4)
        ]
        norm = jnp.zeros((1, lanes), jnp.float32)
        for axis in range(3):
            x = values[axis]
            norm = norm - scale * x * x
            high, mid, low = three(x)
            for row, part in enumerate((high, high, mid, high, low, mid)):
                feature[6 * axis + row:6 * axis + row + 1, :] = part
        feature[18:21, :] = jnp.ones((3, lanes), jnp.float32)
        for row, part in enumerate(three(norm)):
            feature[21 + row:22 + row, :] = part
        for tile in range(lanes // TILE):
            kept = mask[pl.ds(at * (lanes // TILE) + tile, 1), :]
            feature[24:25, tile * TILE:(tile + 1) * TILE] = jnp.broadcast_to(
                jnp.where(kept > 0, 0.0, lowest), (1, TILE)
            )
        near_cost = jnp.dot(
            tgt_side, feature[...].astype(jnp.bfloat16), preferred_element_type=jnp.float32
        )
        mass = jnp.log2(values[3])
        for g in range(batch):
            group = at * batch + g
            span = slice(g * LANES, (g + 1) * LANES)
            cost[group] = near_cost[:, span]
            for axis in range(3):
                points[axis, group // owned, pl.ds(lax.rem(group, owned), 1), :] = (
                    values[axis][:, span]
                )
            masses[group // owned, pl.ds(lax.rem(group, owned), 1), :] = mass[:, span]
        return carried

    lax.fori_loop(0, groups // batch, fetch, 0)
    field[0] = masses[...]

    pl.semaphore_wait(barrier, rows + cols - 2)

    src_log_total = None
    tgt_log_total = None
    tgt_field = None
    for turn in range(passes):
        closing = turn == passes - 1
        send = sends[turn]
        take = takes[turn]
        col_top[...] = jnp.full(col_top.shape, lowest, jnp.float32)
        col_sum[...] = jnp.zeros(col_sum.shape, jnp.float32)

        def visit(peer, piece, turn=turn, closing=closing, send=send):
            base = peer * owned + piece * chunk
            back = jnp.stack([
                jnp.broadcast_to(field[turn, peer, pl.ds(piece * chunk + g, 1), :], (8, LANES))
                for g in range(chunk)
            ])
            unroll = 4

            def tops(at, row_top):
                for sub in range(unroll):
                    span = pl.ds(pl.multiple_of((at * unroll + sub) * 8, 8), 8)
                    d = cost[pl.ds(base, chunk), span, :]
                    row_top = jnp.maximum(row_top, d + term[span, :][None])
                    peak = jnp.max(d + back, axis=0)
                    old = col_top[span, :]
                    new = jnp.maximum(old, peak)
                    col_top[span, :] = new
                    col_sum[span, :] = col_sum[span, :] * jnp.exp2(old - new)
                return row_top

            row_top = lax.fori_loop(
                0, width // (8 * unroll), tops,
                jnp.full((chunk, 8, LANES), 2 * lowest, jnp.float32),
            )
            row_top = jnp.max(row_top, axis=1, keepdims=True)
            tall = jnp.broadcast_to(row_top, (chunk, 8, LANES))

            def sums(at, state):
                for sub in range(unroll):
                    span = pl.ds(pl.multiple_of((at * unroll + sub) * 8, 8), 8)
                    d = cost[pl.ds(base, chunk), span, :]
                    e = jnp.exp2(d + term[span, :][None] - tall)
                    new = [state[0] + e]
                    if closing:
                        for axis in range(3):
                            new.append(state[1 + axis] + e * place[axis, span, :][None])
                    state = tuple(new)
                    col_sum[span, :] += jnp.sum(
                        jnp.exp2(d + back - col_top[span, :][None]), axis=0
                    )
                return state

            nothing = jnp.zeros((chunk, 8, LANES), jnp.float32)
            state = lax.fori_loop(
                0, width // (8 * unroll), sums, (nothing,) * (4 if closing else 1)
            )
            found = [row_top] + [jnp.sum(value, axis=1, keepdims=True) for value in state]
            for entry, value in enumerate(found):
                for g in range(chunk):
                    send[peer, pl.ds(entry * owned + piece * chunk + g, 1), :] = value[g]

        copies = []
        for step in range(1, cols + 1):
            peer = lax.rem(col_at + step, cols)

            def one(piece, carried, peer=peer):
                visit(peer, piece)
                return carried

            lax.fori_loop(0, pieces, one, 0)
            if turn == 0:
                send[peer, 2 * owned:2 * owned + 8, :] = jnp.broadcast_to(tgt_local, (8, LANES))
            if step < cols:
                copy = pltpu.make_async_remote_copy(
                    src_ref=send.at[peer],
                    dst_ref=take.at[step - 1],
                    send_sem=part_out.at[turn, step - 1],
                    recv_sem=part_in.at[turn, step - 1],
                    device_id=(row_at, peer),
                    device_id_type=MESH,
                )
                copy.start()
                copies.append(copy)

        flat_top = col_top[...].T
        flat_sum = col_sum[...].T
        top = jnp.max(flat_top, axis=0, keepdims=True)
        total = jnp.sum(flat_sum * jnp.exp2(flat_top - top), axis=0, keepdims=True)
        for span in range(spans):
            lanes = slice(span * LANES, (span + 1) * LANES)
            col_send[turn, span:span + 1, :] = top[:, lanes]
            col_send[turn, spans + span:spans + span + 1, :] = total[:, lanes]
        rest = 8 - 2 * spans
        col_send[turn, 2 * spans:8, :] = jnp.broadcast_to(src_local, (rest, LANES))
        crossing = []
        for step in range(1, rows):
            copy = pltpu.make_async_remote_copy(
                src_ref=col_send.at[turn],
                dst_ref=col_take.at[turn, step - 1],
                send_sem=cross_out.at[turn, step - 1],
                recv_sem=cross_in.at[turn, step - 1],
                device_id=(lax.rem(row_at + step, rows), col_at),
                device_id_type=MESH,
            )
            copy.start()
            crossing.append(copy)

        for copy in copies:
            copy.wait_recv()
        count = 5 if closing else 2
        top = send[col_at, 0:owned, :]
        for step in range(cols - 1):
            top = jnp.maximum(top, take[step, 0:owned, :])
        merged = [jnp.zeros((owned, LANES), jnp.float32) for _ in range(count - 1)]
        for step in range(cols):
            def read(low, high, step=step):
                if step == cols - 1:
                    return send[col_at, low:high, :]
                return take[step, low:high, :]

            weight = jnp.exp2(read(0, owned) - top)
            merged = [
                value + weight * read((1 + at) * owned, (2 + at) * owned)
                for at, value in enumerate(merged)
            ]
        if turn == 0:
            mass = tgt_local
            for step in range(cols - 1):
                mass = mass + take[step, 2 * owned:2 * owned + 1, :]
            tgt_log_total = jnp.log2(mass)
        fresh = tgt_log_total - top - jnp.log2(merged[0])
        spread = []
        if closing:
            moved[col_at, 0:owned, :] = fresh * (epsilon / log2e)
            for axis in range(3):
                moved[col_at, (1 + axis) * owned:(2 + axis) * owned, :] = (
                    points[axis, col_at] - merged[1 + axis] / merged[0]
                )
            place_of = moved.at[col_at]
        else:
            if turn > 0:
                fresh = 0.5 * (own[...] + fresh)
            own[...] = fresh
            field[turn + 1, col_at] = masses[col_at] + fresh
            place_of = field.at[turn + 1, col_at]
        for step in range(1, cols):
            copy = pltpu.make_async_remote_copy(
                src_ref=place_of,
                dst_ref=place_of,
                send_sem=whole_out.at[turn, step - 1],
                recv_sem=whole_in.at[turn, step - 1],
                device_id=(row_at, lax.rem(col_at + step, cols)),
                device_id_type=MESH,
            )
            copy.start()
            spread.append(copy)

        for copy in crossing:
            copy.wait_recv()
        top = col_send[turn, 0:spans, :]
        for step in range(rows - 1):
            top = jnp.maximum(top, col_take[turn, step, 0:spans, :])
        total = col_send[turn, spans:2 * spans, :] * jnp.exp2(col_send[turn, 0:spans, :] - top)
        for step in range(rows - 1):
            total = total + col_take[turn, step, spans:2 * spans, :] * jnp.exp2(
                col_take[turn, step, 0:spans, :] - top
            )
        if turn == 0:
            mass = col_send[turn, 2 * spans:2 * spans + 1, :]
            for step in range(rows - 1):
                mass = mass + col_take[turn, step, 2 * spans:2 * spans + 1, :]
            src_log_total = jnp.log2(mass)
        fresh = src_log_total - top - jnp.log2(total)
        if closing:
            tgt_out[...] = fresh * (epsilon / log2e)
        else:
            tgt_field = fresh if turn == 0 else 0.5 * (tgt_field + fresh)
            line = jnp.concatenate(
                [tgt_field[span:span + 1, :] for span in range(spans)], axis=1
            )
            term[...] = columns_of(tgt_log + line)

        for copy in spread:
            copy.wait_recv()
        for copy in copies + crossing + spread:
            copy.wait_send()

    for peer in range(cols):
        span = slice(peer * owned, (peer + 1) * owned)
        src_out[span, :] = moved[peer, 0:owned, :]
        for axis in range(3):
            move_out[axis, span, :] = moved[peer, (1 + axis) * owned:(2 + axis) * owned, :]


def local(rows, cols, src_pos, tgt_pos, src_weight, tgt_weight, src_order, tgt_order, tile_mask):
    count = src_pos.shape[1]
    width = tgt_pos.shape[1]
    groups = count // LANES
    owned = groups // cols
    passes = SWEEPS + 2
    f32 = jnp.float32
    vmem = pl.BlockSpec(memory_space=pltpu.VMEM)
    dma = pltpu.SemaphoreType.DMA
    depths = (2 * owned + 8,) + (2 * owned,) * SWEEPS + (5 * owned,)
    src_out, tgt_out, move_out = pl.pallas_call(
        functools.partial(kernel, rows, cols),
        out_shape=(
            jax.ShapeDtypeStruct((groups, LANES), f32),
            jax.ShapeDtypeStruct((width // LANES, LANES), f32),
            jax.ShapeDtypeStruct((3, groups, LANES), f32),
        ),
        in_specs=[vmem] * 7,
        out_specs=(vmem,) * 3,
        scratch_shapes=[
            pltpu.VMEM((4 * LANES, 2 * groups), jnp.bfloat16),
            pltpu.VMEM((FEATURES, 2 * TILE), f32),
            pltpu.VMEM((16, width), f32),
            pltpu.VMEM((LANES, width), f32),
            pltpu.VMEM((3, cols, owned, LANES), f32),
            pltpu.VMEM((cols, owned, LANES), f32),
            pltpu.VMEM((groups, width, LANES), f32),
            pltpu.VMEM((width, LANES), f32),
            pltpu.VMEM((3, width, LANES), f32),
            pltpu.VMEM((width, LANES), f32),
            pltpu.VMEM((width, LANES), f32),
            pltpu.VMEM((passes, cols, owned, LANES), f32),
            pltpu.VMEM((owned, LANES), f32),
            pltpu.VMEM((cols, 4 * owned, LANES), f32),
            *[pltpu.VMEM((cols, depth, LANES), f32) for depth in depths],
            *[pltpu.VMEM((cols - 1, depth, LANES), f32) for depth in depths],
            pltpu.VMEM((passes, 8, LANES), f32),
            pltpu.VMEM((passes, rows - 1, 8, LANES), f32),
            dma((passes, cols - 1)),
            dma((passes, cols - 1)),
            dma((passes, cols - 1)),
            dma((passes, cols - 1)),
            dma((passes, rows - 1)),
            dma((passes, rows - 1)),
        ],
        compiler_params=pltpu.CompilerParams(
            collective_id=0, has_side_effects=True, vmem_limit_bytes=48 * 2**20
        ),
    )(
        src_pos.reshape(3, groups, LANES),
        src_weight.reshape(groups, LANES),
        src_order.reshape(groups, LANES),
        tgt_pos,
        tgt_weight.reshape(1, width),
        tgt_order.reshape(1, width),
        tile_mask,
    )
    return src_out.reshape(count), tgt_out.reshape(width), move_out.reshape(3, count)


def solution(mesh):
    in_specs = (
        P(None, "row"),
        P(None, "col"),
        P("row"),
        P("col"),
        P("row"),
        P("col"),
        P("row", "col"),
    )
    out_specs = (P("row"), P("col"), P(None, "row"))
    body = functools.partial(local, mesh.shape["row"], mesh.shape["col"])
    return jax.shard_map(body, mesh=mesh, in_specs=in_specs, out_specs=out_specs, check_vma=False)
```

time: 551 us -> 94 us (0.17)
  local copies, waits for them, and re-layouts: 187 us -> 4.46 us
  blocking collectives: 174 us -> 0 us
  other arithmetic: 142 us -> 0 us
  Pallas kernels: 0 us -> 88.6 us
  matrix products: 27.8 us -> 0 us
  between operations: 15.9 us -> 0.71 us
    gather x6 -> x0, local copies, waits for them, and re-layouts: 156 us -> none  [the longest x2 90.6 us: local(): src_mass = jnp.take(src_weight, src_order - row_at * rows_here)]
    all_gather x16 -> x0, blocking collectives: 150 us -> none  [merged_2(): gathered = jax.tree.map(lambda a: lax.all_gather(a, axis), part)]
    pallas_call x0 -> x1, Pallas kernels: none -> 88.6 us  [local(): pl.pallas_call(functools.partial(kernel, rows, cols), out_shape=(jax.Shap...]
    reduce_sum x18 -> x0, other arithmetic: 68.1 us -> none  [the longest x16 66.9 us: visit(): row_sum = jnp.sum(row_exp, axis=1)]
    reduce_max x16 -> x0, other arithmetic: 58.5 us -> none  [visit(): row_top = jnp.max(jnp.where(alive, toward, lowest), axis=1)]
    dot_general x4 -> x0, matrix products: 27.8 us -> none  [visit(): pulled = jnp.dot(row_exp, targets.T, precision=lax.Precision.HIGHEST).T]
    psum x2 -> x0, blocking collectives: 23.4 us -> none  [the longest x1 12.4 us: local(): tgt_total = lax.psum(jnp.sum(tgt_mass), 'col')]
    add x69 -> x0, other arithmetic: 10.6 us -> none  [the longest x47 10.1 us: combine(): left_part[member] * left_scale + right_part[member] * right_scale]
  transfers between devices with their start and end apart: 1 -> 0, of which waited for: 0 -> 0; matrix products, arithmetic and copies ran while one was open for 0% -> 0% of each run, Pallas kernels for 0% -> 0%
where the time goes in v1:
time: 94 us; the launch traced here: 93.8 us
  Pallas kernels  88.6 us (94%)
  local copies, waits for them, and re-layouts  4.46 us (5%)
    pallas_call x1, Pallas kernels, local(): pl.pallas_call(functools.partial(kernel, rows, cols), out_shape=(jax.Shap...  88.6 us
    unnamed x17, local copies, waits for them, and re-layouts  4.46 us

profile of v1, /device:TPU:0, one launch (start us, length us, event | category | flops | bytes accessed | tf_op | source)
XLA Modules:
  0.0 93.8 jit_solution(13129187485467316676)
XLA Ops:
  0.6 0.0 copy-start.5
  0.6 0.6 copy-done.5
  1.3 0.1 copy.10.mask
  1.4 0.0 copy-start
  1.4 0.0 copy-start.1
  1.4 0.0 copy-start.2
  1.4 0.0 copy-start.4
  1.4 1.0 %copy.16 = f32[1,3,128,128]{3,2,1,0:T(8,128)S(1)} copy(f32[1,3,128,128]{3,1,2,0:T(4,128)} %bitcast.22) | data formatting | bytes 393216
  2.4 0.0 copy-start.3
  2.5 0.0 copy-done
  2.5 0.0 copy-done.1
  2.5 0.0 copy-done.2
  2.5 0.0 copy-done.4
  2.5 0.6 copy-done.3
  3.1 88.6 %shard_map.94 = (f32[128,128]{1,0:T(8,128)S(1)}, f32[2,128]{1,0:T(2,128)S(1)}, f32[3,128,128]{2,1,0:T(8,128)S(1)}) custom-call(f32[3,128,128]{2,1,0:T(8,128)S(1)} %bitcast.14, f32[128,128]{1,0:T(8,128)S(1)} %bitcast.17, s32[128,128]{1,0:T(8,128)S(1)} %bitcast.18, f32[3,256]{1,0:T(4,128)S(1)} %copy-done.2, f32[1,256]{1,0:T(1,128)S(1)} %bitcast.19, ...), custom_call_target="tpu_custom_call" | custom-call | tf_op jit(solution)/shard_map/pallas_call | solution.py:368
  91.8 0.8 copy.15
  92.6 0.6 copy.19
  93.3 0.6 copy.20
Async XLA Ops:
  0.6 0.7 copy-start.5
  1.4 1.1 %copy-start = (f32[16384]{0:T(1024)S(1)}, f32[16384]{0:T(1024)}, u32[]{:S(2)}) copy-start(f32[16384]{0:T(1024)} %param.9) | copy-start | bytes 196612
  1.4 1.1 %copy-start.1 = (s32[16384]{0:T(1024)S(1)}, s32[16384]{0:T(1024)}, u32[]{:S(2)}) copy-start(s32[16384]{0:T(1024)} %param.11) | copy-start | bytes 196612
  1.4 1.1 %copy-start.2 = (f32[3,256]{1,0:T(4,128)S(1)}, f32[3,256]{1,0:T(4,128)}, u32[]{:S(2)}) copy-start(f32[3,256]{1,0:T(4,128)} %tgt_pos.1) | copy-start | bytes 9220
  1.4 1.1 %copy-start.4 = (s32[256]{0:T(256)S(1)}, s32[256]{0:T(256)}, u32[]{:S(2)}) copy-start(s32[256]{0:T(256)} %param.12) | copy-start | bytes 3076
  2.4 0.7 copy-start.3

commit v2 on v1

--- a/solution.py
+++ b/solution.py
@@ -12,6 +12,7 @@
 SWEEPS = 2
 LANES = 128
 FEATURES = 32
+UNROLL = 32
 
 epsilon = 0.4
 lowest = -1e30
@@ -177,7 +178,7 @@
                 jnp.broadcast_to(field[turn, peer, pl.ds(piece * chunk + g, 1), :], (8, LANES))
                 for g in range(chunk)
             ])
-            unroll = 4
+            unroll = min(UNROLL, width // 8)
 
             def tops(at, row_top):
                 for sub in range(unroll):
@@ -222,28 +223,36 @@
                 for g in range(chunk):
                     send[peer, pl.ds(entry * owned + piece * chunk + g, 1), :] = value[g]
 
-        copies = []
-        for step in range(1, cols + 1):
+        def sending(step, turn=turn, send=send, take=take):
             peer = lax.rem(col_at + step, cols)
-
-            def one(piece, carried, peer=peer):
+            return pltpu.make_async_remote_copy(
+                src_ref=send.at[peer],
+                dst_ref=take.at[step - 1],
+                send_sem=part_out.at[turn, step - 1],
+                recv_sem=part_in.at[turn, step - 1],
+                device_id=(row_at, peer),
+                device_id_type=MESH,
+            )
+
+        def share(step, carried, turn=turn, send=send, sending=sending, visit=visit):
+            peer = lax.rem(col_at + step, cols)
+
+            def one(piece, inner):
                 visit(peer, piece)
-                return carried
+                return inner
 
             lax.fori_loop(0, pieces, one, 0)
             if turn == 0:
                 send[peer, 2 * owned:2 * owned + 8, :] = jnp.broadcast_to(tgt_local, (8, LANES))
-            if step < cols:
-                copy = pltpu.make_async_remote_copy(
-                    src_ref=send.at[peer],
-                    dst_ref=take.at[step - 1],
-                    send_sem=part_out.at[turn, step - 1],
-                    recv_sem=part_in.at[turn, step - 1],
-                    device_id=(row_at, peer),
-                    device_id_type=MESH,
-                )
-                copy.start()
-                copies.append(copy)
+
+            @pl.when(step < cols)
+            def _():
+                sending(step).start()
+
+            return carried
+
+        lax.fori_loop(1, cols + 1, share, 0)
+        copies = [sending(step) for step in range(1, cols)]
 
         flat_top = col_top[...].T
         flat_sum = col_sum[...].T
@@ -376,7 +385,7 @@
         out_specs=(vmem,) * 3,
         scratch_shapes=[
             pltpu.VMEM((4 * LANES, 2 * groups), jnp.bfloat16),
-            pltpu.VMEM((FEATURES, 2 * TILE), f32),
+            pltpu.VMEM((FEATURES, 8 * TILE), f32),
             pltpu.VMEM((16, width), f32),
             pltpu.VMEM((LANES, width), f32),
             pltpu.VMEM((3, cols, owned, LANES), f32),

time: 94 us -> 73.7 us (0.78)
  Pallas kernels: 88.6 us -> 68.3 us
    pallas_call x1, Pallas kernels: 88.6 us -> 68.3 us  [local(): pl.pallas_call(functools.partial(kernel, rows, cols), out_shape=(jax.Shap...]
where the time goes in v2:
time: 73.7 us; the launch traced here: 73.5 us
  Pallas kernels  68.3 us (93%)
  local copies, waits for them, and re-layouts  4.46 us (6%)
    pallas_call x1, Pallas kernels, local(): pl.pallas_call(functools.partial(kernel, rows, cols), out_shape=(jax.Shap...  68.3 us
    unnamed x17, local copies, waits for them, and re-layouts  4.46 us

profile of v2, /device:TPU:0, one launch (start us, length us, event | category | flops | bytes accessed | tf_op | source)
XLA Modules:
  0.0 73.5 jit_solution(18398190840885417792)
XLA Ops:
  0.6 0.0 copy-start.5
  0.6 0.6 copy-done.5
  1.3 0.1 copy.10.mask
  1.4 0.0 copy-start
  1.4 0.0 copy-start.1
  1.4 0.0 copy-start.2
  1.4 0.0 copy-start.4
  1.4 1.0 %copy.16 = f32[1,3,128,128]{3,2,1,0:T(8,128)S(1)} copy(f32[1,3,128,128]{3,1,2,0:T(4,128)} %bitcast.22) | data formatting | bytes 393216
  2.4 0.0 copy-start.3
  2.5 0.0 copy-done
  2.5 0.0 copy-done.1
  2.5 0.0 copy-done.2
  2.5 0.0 copy-done.4
  2.5 0.6 copy-done.3
  3.1 68.3 %shard_map.94 = (f32[128,128]{1,0:T(8,128)S(1)}, f32[2,128]{1,0:T(2,128)S(1)}, f32[3,128,128]{2,1,0:T(8,128)S(1)}) custom-call(f32[3,128,128]{2,1,0:T(8,128)S(1)} %bitcast.14, f32[128,128]{1,0:T(8,128)S(1)} %bitcast.17, s32[128,128]{1,0:T(8,128)S(1)} %bitcast.18, f32[3,256]{1,0:T(4,128)S(1)} %copy-done.2, f32[1,256]{1,0:T(1,128)S(1)} %bitcast.19, ...), custom_call_target="tpu_custom_call" | custom-call | tf_op jit(solution)/shard_map/pallas_call | solution.py:377
  71.5 0.8 %copy.15 = f32[1,3,128,128]{3,1,2,0:T(4,128)} copy(f32[1,3,128,128]{3,2,1,0:T(8,128)S(1)} %bitcast.15) | data formatting | bytes 393216
  72.3 0.6 copy.19
  72.9 0.6 copy.20
Async XLA Ops:
  0.6 0.7 copy-start.5
  1.4 1.1 %copy-start = (f32[16384]{0:T(1024)S(1)}, f32[16384]{0:T(1024)}, u32[]{:S(2)}) copy-start(f32[16384]{0:T(1024)} %param.9) | copy-start | bytes 196612
  1.4 1.1 %copy-start.1 = (s32[16384]{0:T(1024)S(1)}, s32[16384]{0:T(1024)}, u32[]{:S(2)}) copy-start(s32[16384]{0:T(1024)} %param.11) | copy-start | bytes 196612
  1.4 1.1 %copy-start.2 = (f32[3,256]{1,0:T(4,128)S(1)}, f32[3,256]{1,0:T(4,128)}, u32[]{:S(2)}) copy-start(f32[3,256]{1,0:T(4,128)} %tgt_pos.1) | copy-start | bytes 9220
  1.4 1.1 %copy-start.4 = (s32[256]{0:T(256)S(1)}, s32[256]{0:T(256)}, u32[]{:S(2)}) copy-start(s32[256]{0:T(256)} %param.12) | copy-start | bytes 3076
  2.4 0.7 copy-start.3

commit v3 on v2

--- a/solution.py
+++ b/solution.py
@@ -385,7 +385,7 @@
         out_specs=(vmem,) * 3,
         scratch_shapes=[
             pltpu.VMEM((4 * LANES, 2 * groups), jnp.bfloat16),
-            pltpu.VMEM((FEATURES, 8 * TILE), f32),
+            pltpu.VMEM((FEATURES, 16 * TILE), f32),
             pltpu.VMEM((16, width), f32),
             pltpu.VMEM((LANES, width), f32),
             pltpu.VMEM((3, cols, owned, LANES), f32),

time: 73.7 us -> 72.9 us (0.989)
  Pallas kernels: 68.3 us -> 67.5 us
    pallas_call x1, Pallas kernels: 68.3 us -> 67.5 us  [local(): pl.pallas_call(functools.partial(kernel, rows, cols), out_shape=(jax.Shap...]
where the time goes in v3:
time: 72.9 us; the launch traced here: 72.7 us
  Pallas kernels  67.5 us (93%)
  local copies, waits for them, and re-layouts  4.46 us (6%)
    pallas_call x1, Pallas kernels, local(): pl.pallas_call(functools.partial(kernel, rows, cols), out_shape=(jax.Shap...  67.5 us
    unnamed x17, local copies, waits for them, and re-layouts  4.46 us

profile of v3, /device:TPU:0, one launch (start us, length us, event | category | flops | bytes accessed | tf_op | source)
XLA Modules:
  0.0 72.7 jit_solution(4670389021939279552)
XLA Ops:
  0.6 0.0 copy-start.5
  0.6 0.6 copy-done.5
  1.3 0.1 copy.10.mask
  1.4 0.0 copy-start
  1.4 0.0 copy-start.1
  1.4 0.0 copy-start.2
  1.4 0.0 copy-start.4
  1.4 1.0 %copy.16 = f32[1,3,128,128]{3,2,1,0:T(8,128)S(1)} copy(f32[1,3,128,128]{3,1,2,0:T(4,128)} %bitcast.22) | data formatting | bytes 393216
  2.4 0.0 copy-start.3
  2.5 0.0 copy-done
  2.5 0.0 copy-done.1
  2.5 0.0 copy-done.2
  2.5 0.0 copy-done.4
  2.5 0.6 copy-done.3
  3.1 67.5 %shard_map.94 = (f32[128,128]{1,0:T(8,128)S(1)}, f32[2,128]{1,0:T(2,128)S(1)}, f32[3,128,128]{2,1,0:T(8,128)S(1)}) custom-call(f32[3,128,128]{2,1,0:T(8,128)S(1)} %bitcast.14, f32[128,128]{1,0:T(8,128)S(1)} %bitcast.17, s32[128,128]{1,0:T(8,128)S(1)} %bitcast.18, f32[3,256]{1,0:T(4,128)S(1)} %copy-done.2, f32[1,256]{1,0:T(1,128)S(1)} %bitcast.19, ...), custom_call_target="tpu_custom_call" | custom-call | tf_op jit(solution)/shard_map/pallas_call | solution.py:377
  70.7 0.8 %copy.15 = f32[1,3,128,128]{3,1,2,0:T(4,128)} copy(f32[1,3,128,128]{3,2,1,0:T(8,128)S(1)} %bitcast.15) | data formatting | bytes 393216
  71.5 0.6 copy.19
  72.2 0.6 copy.20
Async XLA Ops:
  0.6 0.7 copy-start.5
  1.4 1.1 %copy-start = (f32[16384]{0:T(1024)S(1)}, f32[16384]{0:T(1024)}, u32[]{:S(2)}) copy-start(f32[16384]{0:T(1024)} %param.9) | copy-start | bytes 196612
  1.4 1.1 %copy-start.1 = (s32[16384]{0:T(1024)S(1)}, s32[16384]{0:T(1024)}, u32[]{:S(2)}) copy-start(s32[16384]{0:T(1024)} %param.11) | copy-start | bytes 196612
  1.4 1.1 %copy-start.2 = (f32[3,256]{1,0:T(4,128)S(1)}, f32[3,256]{1,0:T(4,128)}, u32[]{:S(2)}) copy-start(f32[3,256]{1,0:T(4,128)} %tgt_pos.1) | copy-start | bytes 9220
  1.4 1.1 %copy-start.4 = (s32[256]{0:T(256)S(1)}, s32[256]{0:T(256)}, u32[]{:S(2)}) copy-start(s32[256]{0:T(256)} %param.12) | copy-start | bytes 3076
  2.4 0.7 copy-start.3
